TPU v7x, 128 devices: a whole 4x4x4 slice. The times are simulated.
128 devices in a mesh: rows: 32 (over z, x, core), branch: 4 (over y).
Axes of the slice: x: 4, y: 4, z: 4, core: 2. Of those that a mesh axis runs over, the one named last changes fastest.
Arguments:
- logits: bfloat16 [19, 256, 1024], P(None, 'rows'), may hold values from -20 to 360, as said below
- labels: int32 [256, 1024], P('rows'), may hold values from 0 to 18
- pixel_weight: float32 [256, 1024], P('rows'), may hold values from 0.05 to 3.1, as said below
- head_weight: bfloat16 [32, 19], replicated, may hold values from -1.25 to 1.25
- deriv_inner: bfloat16 [4, 32, 8, 32, 1024], P('branch', 'rows'), may hold values from 0.05 to 1, as said below
- deriv_outer: bfloat16 [4, 32, 8, 32, 1024], P('branch', 'rows'), may hold values from 0.05 to 0.7, as said below
- conv_inner: bfloat16 [4, 9, 256, 256], P('branch'), may hold values from -6 to 6
- conv_outer: bfloat16 [4, 9, 256, 256], P('branch'), may hold values from -6 to 6
- join_weight: bfloat16 [4, 4, 256, 256], replicated, may hold values from -6 to 6
Outputs:
- adjoint: float32 [4, 32, 8, 32, 1024], P('branch', 'rows')
Inputs may be any that keep to these rules, and one draw needn't show every extreme that they name: `logits`: saved class scores of the forward pass. `pixel_weight`: positive loss weights. `deriv_inner`: saved derivatives of the inner activation. `deriv_outer`: saved derivatives of the outer activation.
All inputs are finite; a program needn't handle non-finite values.
Results may differ from a plain program's by a relative error of at most 0.022.
Values may be sent and summed in bfloat16 or wider, within the bound.
A program may use at most 192 MiB of HBM per device.

v0:
```python
from functools import partial

import jax
import jax.numpy as jnp
from jax import lax
from jax.sharding import PartitionSpec as P

BASE_CH = 32
BRANCHES = 4
ITERS = 3


def with_halo(block, sides, width):
    for axis, dim in sides:
        count = lax.axis_size(axis)
        forward = [(i, i + 1) for i in range(count - 1)]
        backward = [(target, source) for source, target in forward]
        low = lax.ppermute(
            lax.slice_in_dim(block, block.shape[dim] - width, None, axis=dim), axis, forward
        )
        high = lax.ppermute(lax.slice_in_dim(block, 0, width, axis=dim), axis, backward)
        block = jnp.concatenate([low, block, high], axis=dim)
    return block


def as_sent(array):

    def short(part):
        return part.astype(jnp.bfloat16) if part.dtype == jnp.float32 else part

    return jax.tree.map(short, array)


def local_map(packed, branch_level):
    row_count = packed.shape[0] >> branch_level
    channels = BASE_CH << branch_level
    columns = packed.shape[2] >> branch_level
    return packed[:row_count].reshape(row_count, channels, columns)


def repack(grid_map, total_rows):
    row_count = grid_map.shape[0]
    shaped = grid_map.reshape(row_count, BASE_CH, -1)
    return jnp.pad(shaped, ((0, total_rows - row_count), (0, 0), (0, 0)))


def pool_sum(grid_map, factor):
    height, channels, columns = grid_map.shape
    return grid_map.reshape(height // factor, factor, channels, columns // factor, factor).sum(
        axis=(1, 4)
    )


def coarse_mix(join_weight, source, level_from, level_to):
    mixing = join_weight[level_from, level_to, : BASE_CH << level_from, : BASE_CH << level_to]
    factor_scale = (BASE_CH << level_to) ** (-0.5)
    factor = 2 ** (level_from - level_to)
    mixed = jnp.einsum("oi,roq->riq", mixing, source, preferred_element_type=jnp.float32)
    return (mixed * (factor_scale / (factor * factor))).astype(jnp.bfloat16)


def repeat_up(mixed, factor):
    return jnp.repeat(jnp.repeat(mixed, factor, axis=0), factor, axis=2)


def contribute(join_weight, source, level_from, level_to):
    if level_to < level_from:
        return repeat_up(
            coarse_mix(join_weight, source, level_from, level_to), 2 ** (level_from - level_to)
        )
    mixing = join_weight[level_from, level_to, : BASE_CH << level_from, : BASE_CH << level_to]
    factor_scale = (BASE_CH << level_to) ** (-0.5)
    factor = 2 ** (level_to - level_from)
    pooled = pool_sum(source.astype(jnp.float32), factor)
    mixed = jnp.einsum(
        "oi,roq->riq", mixing.astype(jnp.float32), pooled, precision=lax.Precision.HIGHEST
    )
    return (mixed * factor_scale).astype(jnp.bfloat16)


def conv_level(branch_level, packed, extended, kernels):
    grid_map = local_map(packed, branch_level)
    row_count, channels, columns = grid_map.shape
    above = extended[0].reshape(1, channels, columns)
    below = extended[3].reshape(1, channels, columns)
    padded = jnp.pad(jnp.concatenate([above, grid_map, below], axis=0), ((0, 0), (0, 0), (1, 1)))
    weights = kernels[:, :channels, :channels]
    summed = jnp.zeros((row_count, channels, columns), jnp.float32)
    for kernel_tap in range(9):
        row_shift = kernel_tap // 3 - 1
        col_shift = kernel_tap % 3 - 1
        window = padded[
            1 - row_shift : 1 - row_shift + row_count, :, 1 - col_shift : 1 - col_shift + columns
        ]
        summed = summed + jnp.einsum(
            "oi,roq->riq", weights[kernel_tap], window, preferred_element_type=jnp.float32
        )
    return repack(summed * (9 * channels) ** (-0.5), packed.shape[0])


def send_level(position, join_weight, packed):
    source = local_map(packed, position)
    outgoing = []
    for receiver in range(BRANCHES):
        if receiver == position:
            outgoing.append(jnp.zeros(packed.shape, jnp.bfloat16))
        else:
            outgoing.append(
                repack(contribute(join_weight, source, position, receiver), packed.shape[0])
            )
    return jnp.stack(outgoing)


def rim_rows(packed, branch_level):
    last_row = jnp.right_shift(jnp.int32(packed.shape[0]), branch_level) - 1
    rim_pair = jnp.stack([packed[0], lax.dynamic_index_in_dim(packed, last_row, 0, keepdims=False)])
    return with_halo(rim_pair, (("rows", 0),), 1)


def local_dot(first_vec, second_vec):
    return jnp.sum(first_vec * second_vec)


def on_device(
    logits,
    labels,
    pixel_weight,
    head_weight,
    deriv_inner,
    deriv_outer,
    conv_inner,
    conv_outer,
    join_weight,
):
    branch_level = lax.axis_index("branch")
    deriv_in = deriv_inner[0, 0]
    deriv_out = deriv_outer[0, 0]
    kernels_in = conv_inner[0]
    kernels_out = conv_outer[0]
    probabilities = jax.nn.softmax(logits.astype(jnp.float32), axis=0)
    classes = jnp.arange(logits.shape[0], dtype=jnp.int32)[:, None, None]
    onehot = (labels[None] == classes).astype(jnp.float32)
    prob_error = (pixel_weight[None] * (probabilities - onehot)).astype(jnp.bfloat16)
    first_map = jnp.einsum(
        "ck,khq->hcq", head_weight, prob_error, preferred_element_type=jnp.float32
    )
    loss_source = jnp.where(branch_level == 0, first_map, 0.0)
    iterate = jnp.zeros_like(loss_source)
    previous = loss_source
    update = loss_source
    lefts = []
    rights = []
    for iteration in range(ITERS):
        iterate = iterate + update
        scaled_map = (deriv_out.astype(jnp.float32) * iterate).astype(jnp.bfloat16)
        extended = rim_rows(scaled_map, branch_level)
        inner_map = lax.switch(
            branch_level,
            [partial(conv_level, position) for position in range(BRANCHES)],
            scaled_map,
            extended,
            kernels_out,
        )
        w_map = (deriv_in.astype(jnp.float32) * inner_map).astype(jnp.bfloat16)
        extended_w = rim_rows(w_map, branch_level)
        conv_part = lax.switch(
            branch_level,
            [partial(conv_level, position) for position in range(BRANCHES)],
            w_map,
            extended_w,
            kernels_in,
        )
        outgoing = lax.switch(
            branch_level,
            [partial(send_level, position, join_weight) for position in range(BRANCHES)],
            scaled_map,
        )
        incoming = jax.tree.map(
            lambda part, own: part.astype(own.dtype),
            lax.all_to_all(as_sent(outgoing), "branch", split_axis=0, concat_axis=0, tiled=True),
            outgoing,
        )
        joined = jnp.sum(incoming.astype(jnp.float32), axis=0)
        current = scaled_map.astype(jnp.float32) + conv_part + joined + loss_source - iterate
        change = current - previous
        previous = current
        held_pairs = len(lefts)
        if held_pairs > 0:
            pair_terms = [local_dot(right_vec, change) for right_vec in rights] + [
                local_dot(update, left_vec) for left_vec in lefts
            ]
            pair_sums = lax.psum(jnp.stack(pair_terms), ("rows", "branch"))
            along_right = pair_sums[:held_pairs]
            along_left = pair_sums[held_pairs:]
        right_new = -update
        for slot_index in range(held_pairs):
            right_new = right_new + along_left[slot_index] * rights[slot_index]
        curvature = lax.psum(local_dot(right_new, change), ("rows", "branch"))
        left_new = update + change
        for slot_index in range(held_pairs):
            left_new = left_new - along_right[slot_index] * lefts[slot_index]
        left_new = left_new / curvature
        lefts.append(left_new)
        rights.append(right_new)
        projections = lax.psum(
            jnp.stack([local_dot(right_vec, current) for right_vec in rights]), ("rows", "branch")
        )
        coefficients = [projections[slot_index] for slot_index in range(held_pairs + 1)]
        update = current
        for slot_index in range(len(lefts)):
            update = update - coefficients[slot_index] * lefts[slot_index]
    iterate = iterate + update
    return iterate[None, None]


def solution(mesh):
    placed = (
        P(None, "rows", None),
        P("rows", None),
        P("rows", None),
        P(),
        P("branch", "rows", None, None, None),
        P("branch", "rows", None, None, None),
        P("branch", None, None, None),
        P("branch", None, None, None),
        P(),
    )
    return jax.shard_map(
        on_device,
        mesh=mesh,
        in_specs=placed,
        out_specs=P("branch", "rows", None, None, None),
        check_vma=False,
    )
```

profile of v0, /device:TPU:1, one launch (start us, length us, event | category | flops | bytes accessed | tf_op | source)
XLA Modules:
  0.0 886.7 jit_solution(9029627414032882998)
XLA Ops:
  3.4 2.4 fusion.787
  5.8 44.6 %conditional.11 = (bf16[4,8,32,1024]{3,2,1,0:T(8,128)(2,1)S(1)}) conditional(s32[]{:T(128)} %clamp.2, (bf16[8,32,1024]{2,1,0:T(8,128)(2,1)}, bf16[4,4,256,256]{3,2,1,0:T(8,128)(2,1)S(1)}) %tuple.305, (bf16[8,32,1024]{2,1,0:T(8,128)(2,1)}, bf16[4,4,256,256]{3,2,1,0:T(8,128)(2,1)S(1)}) %tuple.306, ...), branch_computations={%region_10.15_spmd, %region_15.19_spmd, %region_19.22_spmd, %regio... | conditional | flops 92909568 | bytes 17326116 | solution.py:173
  5.8 2.6 copy.423
  8.4 3.8 convert_element_type.379
  12.2 3.4 reduce_sum.248
  16.1 2.1 convert_reduce_fusion
  19.8 6.6 reduce_sum.242
  51.7 48.7 %all-to-all-start = ((bf16[4,8,32,1024]{3,2,1,0:T(8,128)(2,1)}), bf16[4,8,32,1024]{3,2,1,0:T(8,128)(2,1)}, u32[]{:S(2)}, u32[]{:S(2)}) async-start(bf16[4,8,32,1024]{3,2,1,0:T(8,128)(2,1)} %copy-done.31), calls=%async_computation | async-start | bytes 4194304 | tf_op jit(solution)/shard_map/all_to_all | solution.py:180
  100.5 4.0 collective-permute-start
  106.4 4.0 collective-permute-done.1
  110.4 13.1 %conditional.9 = (f32[8,32,1024]{2,1,0:T(8,128)}) conditional(s32[]{:T(128)} %clamp.2, (bf16[1,32,1024]{2,1,0:T(8,128)(2,1)}, bf16[8,32,1024]{2,1,0:T(8,128)(2,1)S(1)}, bf16[1,32,1024]{2,1,0:T(8,128)(2,1)}, bf16[9,256,256]{2,1,0:T(8,128)(2,1)S(1)}) %tuple.309, (bf16[1,32,1024]{2,1,0:T(8,128)(2,1)}, ...), branch_computations={%region_2.3_spmd, %region_3.4_spmd, %region_4.5_spmd, %region_5.6_... | conditional | flops 159391232 | bytes 26420488 | solution.py:157
  127.0 2.4 collective-permute-start.3
  129.5 3.2 collective-permute-done.3
  132.6 14.4 %conditional.10 = (f32[8,32,1024]{2,1,0:T(8,128)}) conditional(s32[]{:T(128)} %clamp.2, (bf16[1,32,1024]{2,1,0:T(8,128)(2,1)S(1)}, bf16[8,32,1024]{2,1,0:T(8,128)(2,1)S(1)}, bf16[1,32,1024]{2,1,0:T(8,128)(2,1)S(1)}, bf16[9,256,256]{2,1,0:T(8,128)(2,1)S(1)}) %tuple.293, (bf16[1,32,1024]{2,1,0:T(8,128)(2,1)S(1)}, ...), branch_computations={%region_6.7_spmd, %region_7.8_spmd, %region_8.9_spmd, %region_9.10... | conditional | flops 159391232 | bytes 33241436 | solution.py:166
  147.0 2.2 convert_reduce_fusion.11
  151.3 77.7 %all-reduce.71 = (f32[]{:T(128)}, f32[]{:T(128)}) all-reduce(f32[]{:T(128)} %get-tuple-element.671, f32[]{:T(128)} %get-tuple-element.670), channel_id=1, replica_groups=mesh['rows'=32,'branch'=4] {'rows','branch'}, use_global_device_ids=true, to_apply=%region_27.28 | all-reduce | flops 2 | bytes 16 | tf_op jit(solution)/shard_map/psum | solution.py:198
  228.9 3.7 fusion.788
  232.7 54.4 %conditional.14 = (bf16[4,8,32,1024]{3,2,1,0:T(8,128)(2,1)}) conditional(s32[]{:T(128)} %clamp.2, (bf16[8,32,1024]{2,1,0:T(8,128)(2,1)}, bf16[4,4,256,256]{3,2,1,0:T(8,128)(2,1)}) %tuple.118, (bf16[8,32,1024]{2,1,0:T(8,128)(2,1)}, bf16[4,4,256,256]{3,2,1,0:T(8,128)(2,1)}) %tuple.118, (bf16[8,32,1024]{2,1,0:T(8,128)(2,1)}, ...), branch_computations={%region_36.41_spmd, %region_41.45_spmd, %region_45.48_spmd, %regio... | conditional | flops 92909568 | bytes 17850432 | solution.py:173
  232.9 2.7 copy.432
  235.5 3.8 convert_element_type.417
  239.3 4.1 reduce_sum.311
  246.5 2.1 convert_reduce_fusion.3
  255.2 6.6 reduce_sum.310
  261.8 2.7 fusion.487
  267.2 2.8 pad_maximum_fusion.35
  287.1 54.6 %all-to-all-start.1 = ((bf16[4,8,32,1024]{3,2,1,0:T(8,128)(2,1)}), bf16[4,8,32,1024]{3,2,1,0:T(8,128)(2,1)}, u32[]{:S(2)}, u32[]{:S(2)}) async-start(bf16[4,8,32,1024]{3,2,1,0:T(8,128)(2,1)} %get-tuple-element.751), calls=%async_computation.1 | async-start | bytes 4194304 | tf_op jit(solution)/shard_map/all_to_all | solution.py:180
  342.6 2.3 collective-permute-start.4
  345.0 2.2 collective-permute-start.5
  347.2 3.8 collective-permute-done.5
  351.0 14.4 %conditional.12 = (f32[8,32,1024]{2,1,0:T(8,128)}) conditional(s32[]{:T(128)} %clamp.2, (bf16[1,32,1024]{2,1,0:T(8,128)(2,1)S(1)}, bf16[8,32,1024]{2,1,0:T(8,128)(2,1)}, bf16[1,32,1024]{2,1,0:T(8,128)(2,1)S(1)}, bf16[9,256,256]{2,1,0:T(8,128)(2,1)S(1)}) %tuple.285, (bf16[1,32,1024]{2,1,0:T(8,128)(2,1)S(1)}, ...), branch_computations={%region_28.29_spmd, %region_29.30_spmd, %region_30.31_spmd, %regio... | conditional | flops 159391232 | bytes 31144256 | solution.py:157
  351.0 2.3 fusion.269
  368.8 2.4 collective-permute-start.7
  371.3 3.2 collective-permute-done.7
  374.4 14.7 %conditional.13 = (f32[8,32,1024]{2,1,0:T(8,128)}) conditional(s32[]{:T(128)} %clamp.2, (bf16[1,32,1024]{2,1,0:T(8,128)(2,1)S(1)}, bf16[8,32,1024]{2,1,0:T(8,128)(2,1)S(1)}, bf16[1,32,1024]{2,1,0:T(8,128)(2,1)S(1)}, bf16[9,256,256]{2,1,0:T(8,128)(2,1)S(1)}) %tuple.297, (bf16[1,32,1024]{2,1,0:T(8,128)(2,1)S(1)}, ...), branch_computations={%region_32.33_spmd, %region_33.34_spmd, %region_34.35_spmd, %regio... | conditional | flops 159391232 | bytes 33241436 | solution.py:166
  389.2 2.3 convert_reduce_fusion.10
  391.5 3.8 multiply_reduce_fusion.11
  396.6 88.3 %psum.58 = f32[2]{0:T(128)S(1)} all-reduce(f32[2]{0:T(128)S(1)} %pad_maximum_fusion.57), channel_id=1, replica_groups=mesh['rows'=32,'branch'=4] {'rows','branch'}, use_global_device_ids=true, to_apply=%region_53.54 | all-reduce | flops 2 | bytes 16 | tf_op jit(solution)/shard_map/psum | solution.py:192
  485.5 5.8 multiply_reduce_fusion.8
  492.7 63.2 %all-reduce.70 = (f32[2]{0:T(128)S(1)}, f32[]{:T(128)}) all-reduce(f32[2]{0:T(128)S(1)} %pad_maximum_fusion.58, f32[]{:T(128)} %get-tuple-element.677), channel_id=1, replica_groups=mesh['rows'=32,'branch'=4] {'rows','branch'}, use_global_device_ids=true, to_apply=%region_55.56 | all-reduce | flops 3 | bytes 24 | tf_op jit(solution)/shard_map/psum | solution.py:205
  556.5 7.5 fusion.789
  564.0 54.3 %conditional.17 = (bf16[4,8,32,1024]{3,2,1,0:T(8,128)(2,1)}) conditional(s32[]{:T(128)} %clamp.2, (bf16[8,32,1024]{2,1,0:T(8,128)(2,1)}, bf16[4,4,256,256]{3,2,1,0:T(8,128)(2,1)}) %tuple.121, (bf16[8,32,1024]{2,1,0:T(8,128)(2,1)}, bf16[4,4,256,256]{3,2,1,0:T(8,128)(2,1)}) %tuple.121, (bf16[8,32,1024]{2,1,0:T(8,128)(2,1)}, ...), branch_computations={%region_66.71_spmd, %region_71.75_spmd, %region_75.78_spmd, %regio... | conditional | flops 92909568 | bytes 17850432 | solution.py:173
  564.4 2.7 copy.441
  567.1 3.8 convert_element_type.455
  570.9 4.1 reduce_sum.332
  578.0 2.1 convert_reduce_fusion.6
  586.8 6.6 reduce_sum.331
  593.3 2.7 fusion.749
  598.8 2.8 pad_maximum_fusion.54
  618.3 53.4 %all-to-all-start.2 = ((bf16[4,8,32,1024]{3,2,1,0:T(8,128)(2,1)}), bf16[4,8,32,1024]{3,2,1,0:T(8,128)(2,1)}, u32[]{:S(2)}, u32[]{:S(2)}) async-start(bf16[4,8,32,1024]{3,2,1,0:T(8,128)(2,1)} %get-tuple-element.754), calls=%async_computation.2 | async-start | bytes 4194304 | tf_op jit(solution)/shard_map/all_to_all | solution.py:180
  672.6 2.8 collective-permute-start.8
  677.3 4.0 collective-permute-done.9
  681.3 13.5 %conditional.15 = (f32[8,32,1024]{2,1,0:T(8,128)S(1)}) conditional(s32[]{:T(128)} %clamp.2, (bf16[1,32,1024]{2,1,0:T(8,128)(2,1)S(1)}, bf16[8,32,1024]{2,1,0:T(8,128)(2,1)}, bf16[1,32,1024]{2,1,0:T(8,128)(2,1)S(1)}, bf16[9,256,256]{2,1,0:T(8,128)(2,1)S(1)}) %tuple.289, (bf16[1,32,1024]{2,1,0:T(8,128)(2,1)S(1)}, ...), branch_computations={%region_58.59_spmd, %region_59.60_spmd, %region_60.61_spmd, %regio... | conditional | flops 159391232 | bytes 31144256 | solution.py:157
  681.3 2.3 fusion.531
  698.0 2.4 collective-permute-start.11
  700.4 3.2 collective-permute-done.11
  703.6 12.5 %conditional.16 = (f32[8,32,1024]{2,1,0:T(8,128)S(1)}) conditional(s32[]{:T(128)} %clamp.2, (bf16[1,32,1024]{2,1,0:T(8,128)(2,1)S(1)}, bf16[8,32,1024]{2,1,0:T(8,128)(2,1)S(1)}, bf16[1,32,1024]{2,1,0:T(8,128)(2,1)S(1)}, bf16[9,256,256]{2,1,0:T(8,128)(2,1)S(1)}) %tuple.301, (bf16[1,32,1024]{2,1,0:T(8,128)(2,1)S(1)}, ...), branch_computations={%region_62.63_spmd, %region_63.64_spmd, %region_64.65_spmd, %regio... | conditional | flops 159391232 | bytes 30614848 | solution.py:166
  717.1 2.3 convert_reduce_fusion.9
  719.4 4.4 multiply_reduce_fusion.4
  723.8 4.4 multiply_reduce_fusion.3
  728.2 2.7 pad_maximum_fusion.59
  730.9 73.8 %psum.61 = f32[4]{0:T(128)S(1)} all-reduce(f32[4]{0:T(128)S(1)} %pad_maximum_fusion.59), channel_id=1, replica_groups=mesh['rows'=32,'branch'=4] {'rows','branch'}, use_global_device_ids=true, to_apply=%region_86.87 | all-reduce | flops 4 | bytes 32 | tf_op jit(solution)/shard_map/psum | solution.py:192
  805.4 4.6 multiply_reduce_fusion.6
  811.9 64.1 %all-reduce.69 = (f32[]{:T(128)}, f32[3]{0:T(128)S(1)}) all-reduce(f32[]{:T(128)} %get-tuple-element.675, f32[3]{0:T(128)S(1)} %pad_maximum_fusion.60), channel_id=1, replica_groups=mesh['rows'=32,'branch'=4] {'rows','branch'}, use_global_device_ids=true, to_apply=%region_90.91 | all-reduce | flops 4 | bytes 32 | tf_op jit(solution)/shard_map/psum | solution.py:198
  876.6 9.9 %add_bitcast_fusion = f32[1,1,8,32,1024]{4,3,2,1,0:T(8,128)} fusion(f32[8,32,1024]{2,1,0:T(8,128)} %get-tuple-element.692, f32[8,32,1024]{2,1,0:T(8,128)} %copy-done.25, f32[8,32,1024]{2,1,0:T(8,128)} %copy-done.26, f32[]{:T(128)} %get-tuple-element.682, f32[]{:T(128)} %bitcast.647, f32[]{:T(128)} %bitcast.646, f32[]{:T(128)} %bitcast.645, f32[]{:T(128)} %bitcast.644, ...), kind=kLoop, calls=%fused_computation.1302 | loop fusion | flops 6291456 | bytes 7340072 | tf_op jit(solution)/shard_map/broadcast_in_dim | solution.py:213
  (196 shorter events, 137.2 us)
Async XLA Ops:
  0.0 3.3 copy-start
  3.3 2.4 copy-start.4
  50.4 1.3 copy-start.31
  51.7 48.7 %copy-start.8 = (bf16[8,32,1024]{2,1,0:T(8,128)(2,1)S(1)}, bf16[8,32,1024]{2,1,0:T(8,128)(2,1)}, u32[]{:S(2)}) copy-start(bf16[8,32,1024]{2,1,0:T(8,128)(2,1)} %get-tuple-element.744) | copy-start | bytes 1572868
  51.7 58.7 %copy-start.2 = (bf16[1,9,256,256]{3,2,1,0:T(8,128)(2,1)S(1)}, bf16[1,9,256,256]{3,2,1,0:T(8,128)(2,1)}, u32[]{:S(2)}) copy-start(bf16[1,9,256,256]{3,2,1,0:T(8,128)(2,1)} %param.52) | copy-start | bytes 3538948
  51.7 95.3 %all-to-all-start = ((bf16[4,8,32,1024]{3,2,1,0:T(8,128)(2,1)}), bf16[4,8,32,1024]{3,2,1,0:T(8,128)(2,1)}, u32[]{:S(2)}, u32[]{:S(2)}) async-start(bf16[4,8,32,1024]{3,2,1,0:T(8,128)(2,1)} %copy-done.31), calls=%async_computation | async-start | bytes 4194304 | tf_op jit(solution)/shard_map/all_to_all | solution.py:180
  100.5 5.9 collective-permute-start
  104.4 6.0 collective-permute-start.1
  123.5 9.1 %copy-start.3 = (bf16[1,9,256,256]{3,2,1,0:T(8,128)(2,1)S(1)}, bf16[1,9,256,256]{3,2,1,0:T(8,128)(2,1)}, u32[]{:S(2)}) copy-start(bf16[1,9,256,256]{3,2,1,0:T(8,128)(2,1)} %param.51) | copy-start | bytes 3538948
  125.1 4.3 collective-permute-start.2
  127.0 5.6 collective-permute-start.3
  132.6 0.8 copy-start.18
  136.2 1.5 copy-start.19
  137.7 1.1 copy-start.12
  147.0 2.2 copy-start.22
  147.0 2.2 copy-start.36
  287.1 102.0 %all-to-all-start.1 = ((bf16[4,8,32,1024]{3,2,1,0:T(8,128)(2,1)}), bf16[4,8,32,1024]{3,2,1,0:T(8,128)(2,1)}, u32[]{:S(2)}, u32[]{:S(2)}) async-start(bf16[4,8,32,1024]{3,2,1,0:T(8,128)(2,1)} %get-tuple-element.751), calls=%async_computation.1 | async-start | bytes 4194304 | tf_op jit(solution)/shard_map/all_to_all | solution.py:180
  342.6 4.5 collective-permute-start.4
  345.0 6.0 collective-permute-start.5
  354.7 1.5 copy-start.9
  356.3 1.1 copy-start.13
  366.9 4.3 collective-permute-start.6
  368.8 5.6 collective-permute-start.7
  374.6 0.8 copy-start.20
  378.2 1.5 copy-start.21
  379.7 1.1 copy-start.14
  389.1 2.3 copy-start.5
  389.1 2.3 copy-start.23
  389.2 2.3 copy-start.37
  618.3 98.8 %all-to-all-start.2 = ((bf16[4,8,32,1024]{3,2,1,0:T(8,128)(2,1)}), bf16[4,8,32,1024]{3,2,1,0:T(8,128)(2,1)}, u32[]{:S(2)}, u32[]{:S(2)}) async-start(bf16[4,8,32,1024]{3,2,1,0:T(8,128)(2,1)} %get-tuple-element.754), calls=%async_computation.2 | async-start | bytes 4194304 | tf_op jit(solution)/shard_map/all_to_all | solution.py:180
  672.6 4.7 collective-permute-start.8
  675.3 6.0 collective-permute-start.9
  685.1 1.5 copy-start.7
  686.6 1.1 copy-start.15
  696.1 4.3 collective-permute-start.10
  698.0 5.6 collective-permute-start.11
  704.1 0.8 copy-start.16
  706.8 1.1 copy-start.17
  716.1 1.0 copy-start.38
  717.1 2.3 copy-start.6
  717.1 2.3 copy-start.11
  717.1 2.3 copy-start.24
  719.4 4.4 copy-start.10
  723.8 4.4 copy-start.25
  723.8 4.4 copy-start.26
  876.6 9.9 %copy-start.1 = (bf16[32,19]{0,1:T(8,128)(2,1)S(1)}, bf16[32,19]{0,1:T(8,128)(2,1)}, u32[]{:S(2)}) copy-start(bf16[32,19]{0,1:T(8,128)(2,1)} %param.48) | copy-start | bytes 3652
where the time goes:
time: 900 us; the launch traced here: 887 us
  blocking collectives  367 us (41%)
  starting transfers between devices  185 us (21%)
  other arithmetic  133 us (15%)
  matrix products  76 us (8%)
  loops' own time  56.9 us (6%)
  local copies, waits for them, and re-layouts  47 us (5%)
  waiting for transfers between devices  21.4 us (2%)
    psum x2, blocking collectives, on_device(): pair_sums = lax.psum(jnp.stack(pair_terms), ('rows', 'branch'))  162 us
    all_to_all x3, starting transfers between devices, on_device(): lax.all_to_all(as_sent(outgoing), 'branch', split_axis=0, concat_axis=0,...  157 us
    psum x2, blocking collectives, on_device(): curvature = lax.psum(local_dot(right_new, change), ('rows', 'branch'))  142 us
    psum x1, blocking collectives, on_device(): lax.psum(jnp.stack([local_dot(right_vec, current) for right_vec in rights...  63.2 us
    dot_general x54, matrix products, conv_level(): jnp.einsum('oi,roq->riq', weights[kernel_tap], window, preferred_element_...  60.4 us
    another operation x3, loops' own time, on_device(): lax.switch(branch_level, [partial(send_level, position, join_weight) for...  55.1 us
    reduce_sum x12, other arithmetic, pool_sum(): grid_map.reshape(height // factor, factor, channels, columns // factor, f...  38.1 us
    reduce_sum x6, other arithmetic, local_dot(): return jnp.sum(first_vec * second_vec)  25 us
  transfers between devices with their start and end apart: 15, of which 6 were waited for; matrix products, arithmetic and copies ran while one was open for 9% of the time, Pallas kernels for 0%

commit v1 on v0

v1 whole, which is shorter than its diff:
```python
from functools import partial

import jax
import jax.numpy as jnp
from jax import lax
from jax.experimental import pallas as pl
from jax.experimental.pallas import tpu as pltpu
from jax.sharding import PartitionSpec as P

BASE_CH = 32
BRANCHES = 4
ITERS = 3
GROUP = (6, 2, 1, 1)
MESH = pl.DeviceIdType.MESH
BF16 = jnp.bfloat16
F32 = jnp.float32


def dot(left, right):
    return jnp.dot(left, right, preferred_element_type=F32)


def dot_nt(left, right):
    return lax.dot_general(left, right, (((1,), (1,)), ((), ())), preferred_element_type=F32)


def iotas(shape):
    return lax.broadcasted_iota(jnp.int32, shape, 0), lax.broadcasted_iota(jnp.int32, shape, 1)


def flags(mask):
    return jnp.where(mask, 1.0, 0.0).astype(BF16)


def shift_cols(values, by):
    width = values.shape[1]
    _, col = iotas(values.shape)
    if by == 1:
        return jnp.where(col == 0, 0.0, pltpu.roll(values, 1, 1))
    return jnp.where(col == width - 1, 0.0, pltpu.roll(values, width - 1, 1))


def wait_all(ref, sem):
    pltpu.make_async_copy(ref, ref, sem).wait()


def kernel(
    pieces,
    across,
    logits,
    labels,
    pixel_weight,
    head_weight,
    deriv_inner,
    deriv_outer,
    conv_inner,
    conv_outer,
    join_weight,
    out,
    s_logits,
    s_labels,
    s_pixel,
    s_head,
    outer,
    inner,
    k_outer,
    k_inner,
    k_join,
    band0,
    band1,
    band2,
    band3,
    mix,
    pool2,
    pool4,
    pool8,
    up2,
    up4,
    up8,
    scaled,
    wmap,
    vecs,
    give01,
    give02,
    give03,
    give12,
    give13,
    give23,
    take01,
    take02,
    take03,
    take12,
    take13,
    take23,
    part,
    took_pair,
    part_pair,
    took,
    in_sem,
    rim_send,
    rim_recv,
    halo_send,
    halo_recv,
    join_send,
    join_recv,
    sum_send,
    sum_recv,
):
    piece = lax.axis_index("rows")
    branch = lax.axis_index("branch")
    full_rows, width = outer.shape[0], outer.shape[2]
    row_count = jnp.right_shift(jnp.int32(full_rows), branch)
    bands = (band0, band1, band2, band3)
    gives = {(0, 1): give01, (0, 2): give02, (0, 3): give03, (1, 2): give12, (1, 3): give13, (2, 3): give23}
    takes = {(0, 1): take01, (0, 2): take02, (0, 3): take03, (1, 2): take12, (1, 3): take13, (2, 3): take23}
    has_above = piece > 0
    has_below = piece < pieces - 1
    core, chip_x, chip_z = lax.rem(piece, 2), lax.rem(piece // 2, across), piece // (2 * across)
    deep = pieces // (2 * across)

    def sizes(level):
        return full_rows >> level, BASE_CH << level, width >> level, 1 << level

    def hops(offset):
        return sum(min(step, size - step) for step, size in zip(offset, (across, deep, BRANCHES)))

    offsets = [
        (x, z, y) for x in range(across) for z in range(deep) for y in range(BRANCHES) if x or z or y
    ]
    offsets.sort(key=hops, reverse=True)
    partner = (piece + 1 - 2 * core, branch)

    def chip_peer(offset):
        x = lax.rem(chip_x + offset[0], across)
        z = lax.rem(chip_z + offset[1], deep)
        return ((z * across + x) * 2 + core, lax.rem(branch + offset[2], BRANCHES))

    near = [(lax.rem(piece + step, pieces), branch) for step in (1, 2, pieces - 2, pieces - 1)]
    greeted = [chip_peer(offset) for offset in offsets] + near + [partner]

    def on(level):
        return pl.when(branch == level)

    def input_copies(level):
        rows, chans, _, _ = sizes(level)
        lanes = max(chans, 128)
        pairs = []
        if level == 0:
            pairs += [(logits, s_logits), (labels, s_labels), (pixel_weight, s_pixel), (head_weight, s_head)]
        pairs += [
            (deriv_outer.at[0, 0, pl.ds(0, rows)], outer.at[pl.ds(0, rows)]),
            (conv_outer.at[0, :, pl.ds(0, chans), pl.ds(0, lanes)], k_outer.at[:, pl.ds(0, chans), pl.ds(0, lanes)]),
            (conv_inner.at[0, :, pl.ds(0, chans), pl.ds(0, lanes)], k_inner.at[:, pl.ds(0, chans), pl.ds(0, lanes)]),
            (deriv_inner.at[0, 0, pl.ds(0, rows)], inner.at[pl.ds(1, rows)]),
        ]
        for other in range(level):
            few = BASE_CH << other
            pairs.append((join_weight.at[level, other, pl.ds(0, chans)], k_join.at[other, pl.ds(0, chans)]))
            pairs.append((join_weight.at[other, level, pl.ds(0, few)], k_join.at[3 + other, pl.ds(0, few)]))
        return [pltpu.make_async_copy(src, dst, in_sem.at[at]) for at, (src, dst) in enumerate(pairs)]

    for level in range(BRANCHES):

        @on(level)
        def _(level=level):
            for copy in input_copies(level):
                copy.start()

    barrier = pltpu.get_barrier_semaphore()
    for peer in greeted:
        pl.semaphore_signal(barrier, inc=1, device_id=peer, device_id_type=MESH)

    for ref, factor in ((pool2, 2), (pool4, 4), (pool8, 8)):
        row, col = iotas(ref.shape)
        ref[...] = flags(row // factor == col)
    for ref, factor in ((up2, 2), (up4, 4), (up8, 8)):
        row, col = iotas(ref.shape)
        ref[...] = flags(row == col // factor)

    @pl.when(jnp.logical_not(has_above))
    def _():
        inner[0] = jnp.zeros(inner.shape[1:], BF16)
        for turn in range(ITERS):
            for slot in (0, 1):
                scaled[turn, slot] = jnp.zeros(inner.shape[1:], BF16)

    for level in range(BRANCHES):
        rows = sizes(level)[0]

        @pl.when(jnp.logical_and(branch == level, jnp.logical_not(has_below)))
        def _(rows=rows):
            inner[rows + 1] = jnp.zeros(inner.shape[1:], BF16)
            for turn in range(ITERS):
                for slot in (rows + 2, rows + 3):
                    scaled[turn, slot] = jnp.zeros(inner.shape[1:], BF16)

    @pl.when(jnp.logical_and(branch == 3, piece == 1))
    def _():
        for turn in range(ITERS):
            scaled[turn, 0] = jnp.zeros(inner.shape[1:], BF16)

    @pl.when(jnp.logical_and(branch == 3, piece == pieces - 2))
    def _():
        for turn in range(ITERS):
            scaled[turn, 4] = jnp.zeros(inner.shape[1:], BF16)

    def shuffle(level):
        chans, factor = BASE_CH << level, 1 << level
        row, col = iotas((chans, chans))
        return flags(col == factor * lax.rem(row, BASE_CH) + row // BASE_CH)

    def prepare(level):
        rows, chans, _, _ = sizes(level)
        many = GROUP[level]
        order = shuffle(level)
        for which, kernels in enumerate((k_outer, k_inner)):
            for dx in range(3):
                taps = [kernels[3 * dy + dx, :chans, :chans] for dy in (2, 1, 0)]
                if level > 0:
                    taps = [dot(order, tap).astype(BF16) for tap in taps]
                line = dot_nt(order, jnp.concatenate(taps, axis=0)).astype(BF16)
                if many == 1:
                    bands[level][which, dx * chans : (dx + 1) * chans, :] = line
                else:
                    for row_out in range(many):
                        at, to = iotas((3 * chans, (many + 2) * chans))
                        placed = dot(line, flags(to == at + row_out * chans))
                        start = (dx * many + row_out) * chans
                        bands[level][which, start : start + chans, :] = placed.astype(BF16)
        for other in range(level):
            few = BASE_CH << other
            sent = dot(order, k_join[other, :chans, :few]).astype(BF16)
            mix[other, :few, :chans] = dot_nt(shuffle(other), sent).astype(BF16)
            got = dot(shuffle(other), k_join[3 + other, :few, :chans]).astype(BF16)
            mix[3 + other, :chans, :few] = dot_nt(order, got).astype(BF16)

    @on(0)
    def _():
        for copy in input_copies(0)[:5]:
            copy.wait()
        scores = s_logits[...].astype(F32)
        powers = jnp.exp(scores - jnp.max(scores, axis=0, keepdims=True))
        shares = powers / jnp.sum(powers, axis=0, keepdims=True)
        classes = lax.broadcasted_iota(jnp.int32, scores.shape, 0)
        hits = jnp.where(s_labels[...][None] == classes, 1.0, 0.0)
        err = s_pixel[...][None] * (shares - hits)
        count = scores.shape[0]
        flat = err.reshape(count * full_rows, width).astype(BF16)
        row, col = iotas((full_rows * BASE_CH, BASE_CH))
        tall = dot_nt(flags(lax.rem(row, BASE_CH) == col), s_head[...]).astype(BF16)
        row, col = iotas((count, count * full_rows))
        wide = dot(tall, flags(row == col // full_rows))
        row, col = iotas(wide.shape)
        head = jnp.where(row // BASE_CH == lax.rem(col, full_rows), wide, 0.0).astype(BF16)
        first = dot(head, flat)
        for row in range(full_rows):
            own = first[row * BASE_CH : (row + 1) * BASE_CH]
            vecs[0, row] = own
            scaled[0, 2 + row] = (outer[row].astype(F32) * own).astype(BF16)

    @pl.when(branch > 0)
    def _():
        def clear(row, _):
            vecs[0, row] = jnp.zeros(vecs.shape[2:], F32)
            return 0

        lax.fori_loop(0, row_count, clear, 0)

    pl.semaphore_wait(barrier, len(greeted))

    def rim_copy(level, below):
        rows = sizes(level)[0]
        if below:
            return pltpu.make_async_remote_copy(
                deriv_inner.at[0, 0, rows - 1], inner.at[0], rim_send.at[0], rim_recv.at[0],
                device_id=(piece + 1, branch), device_id_type=MESH,
            )
        return pltpu.make_async_remote_copy(
            deriv_inner.at[0, 0, 0], inner.at[rows + 1], rim_send.at[1], rim_recv.at[1],
            device_id=(piece - 1, branch), device_id_type=MESH,
        )

    def send_rim(level):
        @pl.when(has_below)
        def _():
            rim_copy(level, True).start()

        @pl.when(has_above)
        def _():
            rim_copy(level, False).start()

    def wait_rim(level):
        rows = sizes(level)[0]

        @pl.when(has_above)
        def _():
            wait_all(inner.at[0], rim_recv.at[0])

        @pl.when(has_below)
        def _():
            wait_all(inner.at[rows + 1], rim_recv.at[1])

    def halo_copies(level, turn):
        rows = sizes(level)[0]
        if level < 3:
            plan = [
                (1, slice(rows, rows + 2), slice(0, 2)),
                (-1, slice(2, 4), slice(rows + 2, rows + 4)),
            ]
        else:
            plan = [
                (1, slice(2, 3), slice(1, 2)),
                (-1, slice(2, 3), slice(3, 4)),
                (2, slice(2, 3), slice(0, 1)),
                (-2, slice(2, 3), slice(4, 5)),
            ]
        result = []
        for at, (step, src, dst) in enumerate(plan):
            there = piece + step
            source = piece - step
            copy = pltpu.make_async_remote_copy(
                scaled.at[turn, pl.ds(src.start, src.stop - src.start)],
                scaled.at[turn, pl.ds(dst.start, dst.stop - dst.start)],
                halo_send.at[turn, at],
                halo_recv.at[turn, at],
                device_id=(there, branch),
                device_id_type=MESH,
            )
            sends = there < pieces if step > 0 else there >= 0
            gets = source >= 0 if step > 0 else source < pieces
            result.append((sends, copy, gets))
        return result

    def send_halo(level, turn):
        for sends, copy, _ in halo_copies(level, turn):

            @pl.when(sends)
            def _(copy=copy):
                copy.start()

    def join_copy(level, other, turn):
        pair = (min(level, other), max(level, other))
        return pltpu.make_async_remote_copy(
            gives[pair].at[turn], takes[pair].at[turn], join_send.at[turn, other], join_recv.at[turn, level],
            device_id=(piece, jnp.int32(other)), device_id_type=MESH,
        )

    def chunks(block, level):
        span = width >> level
        return [block[:, at * span : (at + 1) * span] for at in range(1 << level)]

    def grid_rows(load, slots, level):
        return jnp.concatenate([part for slot in slots for part in chunks(load(slot), level)], axis=0)

    def send_terms(level, turn):
        rows, chans, cols, _ = sizes(level)
        load = lambda slot: scaled[turn, slot]
        own = grid_rows(load, range(2, 2 + rows), level)
        for other in range(level + 1, BRANCHES):
            factor = 1 << (other - level)
            height, less = rows // factor, cols // factor
            ref = gives[(level, other)]
            if factor == 2:
                spans = [(at, pool2[...]) for at in range(cols // 256)]
                pieces_of = [dot(own[:, at * 256 : (at + 1) * 256], mat) for at, mat in spans]
            else:
                mat = pool4[:cols, :less] if factor == 4 else pool8[:cols, :less]
                pieces_of = [dot(own, mat)]
            for at, part in enumerate(pieces_of):
                span = part.shape[1]
                for row in range(height):
                    summed = part[row * factor * chans : (row * factor + 1) * chans]
                    for extra in range(1, factor):
                        start = (row * factor + extra) * chans
                        summed = summed + part[start : start + chans]
                    ref[turn, row * chans : (row + 1) * chans, at * span : (at + 1) * span] = summed.astype(BF16)
            join_copy(level, other, turn).start()
        for other in range(level):
            few = BASE_CH << other
            factor = 1 << (level - other)
            scale = few ** (-0.5) / (factor * factor)
            ref = gives[(other, level)]
            matrix = mix[other, :few, :chans]
            for row in range(rows):
                mixed = dot(matrix, own[row * chans : (row + 1) * chans])
                ref[turn, row * few : (row + 1) * few, :] = (mixed * scale).astype(BF16)
            join_copy(level, other, turn).start()

    def conv(level, which, load, first, many):
        _, chans, _, _ = sizes(level)
        most = GROUP[level]
        band = bands[level]
        right = grid_rows(load, range(first, first + many + 2), level)
        if many == most:
            left = band[which]
        else:
            left = jnp.concatenate(
                [
                    band[which, dx * most * chans : (dx * most + many) * chans, : (many + 2) * chans]
                    for dx in range(3)
                ],
                axis=0,
            )
        prod = dot(left, right)
        size = many * chans
        return prod[size : 2 * size] + shift_cols(prod[2 * size :], 1) + shift_cols(prod[:size], -1)

    def conv_lanes(level, which, load, first, many):
        _, chans, cols, _ = sizes(level)
        right = jnp.concatenate(
            [grid_rows(load, range(first + at, first + at + 3), level) for at in range(many)], axis=1
        )
        prod = dot(bands[level][which], right)
        result = []
        for at in range(many):
            own = prod[:, at * cols : (at + 1) * cols]
            result.append(
                own[chans : 2 * chans] + shift_cols(own[2 * chans :], 1) + shift_cols(own[:chans], -1)
            )
        return result

    def put_w(level, row, values):
        _, chans, cols, factor = sizes(level)
        scale = (9 * chans) ** (-0.5)
        for at in range(factor):
            lanes = slice(at * cols, (at + 1) * cols)
            part = values[at * BASE_CH : (at + 1) * BASE_CH] * scale
            wmap[row + 1, :, lanes] = (inner[row + 1, :, lanes].astype(F32) * part).astype(BF16)

    def put_out(level, turn, to, row, values):
        _, chans, cols, factor = sizes(level)
        scale = (9 * chans) ** (-0.5)
        for at in range(factor):
            lanes = slice(at * cols, (at + 1) * cols)
            part = values[at * BASE_CH : (at + 1) * BASE_CH] * scale
            vecs[to, row, :, lanes] = scaled[turn, 2 + row, :, lanes].astype(F32) + part

    def outer_conv(level, turn, starts):
        chans = BASE_CH << level
        load = lambda slot: scaled[turn, slot]
        for first, many in starts:
            if level == 3:
                for at, values in enumerate(conv_lanes(level, 0, load, first + 1, many)):
                    put_w(level, first + at, values)
            else:
                values = conv(level, 0, load, first + 1, many)
                for at in range(many):
                    put_w(level, first + at, values[at * chans : (at + 1) * chans])

    def inner_conv(level, turn, to, starts):
        chans = BASE_CH << level
        load = lambda slot: wmap[slot]
        for first, many in starts:
            if level == 3:
                for at, values in enumerate(conv_lanes(level, 1, load, first, many)):
                    put_out(level, turn, to, first + at, values)
            else:
                values = conv(level, 1, load, first, many)
                for at in range(many):
                    put_out(level, turn, to, first + at, values[at * chans : (at + 1) * chans])

    inside = ([(1, 6)], [(1, 2)], [], [])
    edges = ([(-1, 2), (7, 2)], [(-1, 2), (3, 2)], [(-1, 1), (0, 1), (1, 1), (2, 1)], [(-1, 3)])
    early = ([(2, 4)], [], [], [])
    finals = ([(0, 2), (6, 2)], [(0, 2), (2, 2)], [(0, 1), (1, 1)], [(0, 1)])
    order = ((0, 1, 6, 7, 2, 3, 4, 5), (0, 1, 2, 3), (0, 1), (0,))
    rims = (4, 4, 2, 1)

    def convs_before(level, turn, to):
        outer_conv(level, turn, inside[level])
        inner_conv(level, turn, to, early[level])

    def convs_after(level, turn, to):
        for _, copy, gets in halo_copies(level, turn):

            @pl.when(gets)
            def _(copy=copy):
                copy.wait_recv()

        outer_conv(level, turn, edges[level])
        inner_conv(level, turn, to, finals[level])

    def term_rows(level, other, turn):
        rows, chans, cols, _ = sizes(level)
        pair = (min(level, other), max(level, other))
        ref = takes[pair]
        wait_all(ref.at[turn], join_recv.at[turn, other])
        if other < level:
            less = BASE_CH << other
            matrix = mix[3 + other, :chans, :less]
            scale = chans ** (-0.5)
            mixed = [dot(matrix, ref[turn, row * less : (row + 1) * less, :]) for row in range(rows)]
            return [(value * scale).astype(BF16).astype(F32) for value in mixed]
        times = 1 << (other - level)
        got = ref[turn]
        if times == 2:
            wide = jnp.concatenate(
                [dot(got[:, at * 128 : (at + 1) * 128], up2[...]) for at in range(cols // 256)], axis=1
            )
        else:
            wide = dot(got, up4[: cols // 4, :cols] if times == 4 else up8[: cols // 8, :cols])
        starts = [(row // times) * chans for row in range(rows)]
        return [wide[start : start + chans] for start in starts]

    def finish(level, turn):
        _, _, cols, factor = sizes(level)
        to = turn + 1
        others = [other for other in range(BRANCHES) if other != level and (turn > 0 or other == 0)]
        terms = [term_rows(level, other, turn) for other in others]
        for done, row in enumerate(order[level]):
            for at in range(factor):
                lanes = slice(at * cols, (at + 1) * cols)
                parts = [] if level > 0 and turn == 0 else [vecs[to, row, :, lanes]]
                parts += [term[row][at * BASE_CH : (at + 1) * BASE_CH] for term in terms]
                value = parts[0]
                for more in parts[1:]:
                    value = value + more
                vecs[to, row, :, lanes] = value
                if to < ITERS:
                    scaled[to, 2 + row, :, lanes] = (outer[row, :, lanes].astype(F32) * value).astype(BF16)
            if to < ITERS and done + 1 == rims[level]:
                send_halo(level, to)

    def products(pairs):
        def step(row, sums):
            result = []
            for have, (left, right) in zip(sums, pairs):
                prod = vecs[left, row] * vecs[right, row]
                result.append(have + ((prod[0:8] + prod[8:16]) + (prod[16:24] + prod[24:32])))
            return tuple(result)

        zero = jnp.zeros((8, width), F32)
        sums = lax.fori_loop(0, row_count, step, (zero,) * len(pairs))
        lane = lax.broadcasted_iota(jnp.int32, part.shape, 1)
        row_of = part[...]
        for value, (left, right) in zip(sums, pairs):
            whole = jnp.sum(jnp.sum(value, axis=0, keepdims=True), axis=1, keepdims=True)
            row_of = row_of + jnp.where(lane == 3 * left + right, whole, 0.0)
        part[...] = row_of

    part[...] = jnp.zeros(part.shape, F32)

    def pair_copy():
        return pltpu.make_async_remote_copy(
            part, took_pair, sum_send.at[0], sum_recv.at[0], device_id=partner, device_id_type=MESH
        )

    def last_step():
        products([(0, 3), (1, 3), (2, 3)])
        copy = pair_copy()
        copy.start()
        copy.wait_recv()
        part_pair[...] = part[...] + took_pair[...]
        for at, offset in enumerate(offsets):
            pltpu.make_async_remote_copy(
                part_pair, took.at[at], sum_send.at[1], sum_recv.at[1],
                device_id=chip_peer(offset), device_id_type=MESH,
            ).start()
        wait_all(took, sum_recv.at[1])
        sums = part_pair[...] + jnp.sum(took[...], axis=0)

        def gram(left, right):
            at = 3 * left + right
            return sums[:, at : at + 1]

        g00, g01, g02, g03 = (gram(0, at) for at in range(4))
        g11, g12, g13 = (gram(1, at) for at in range(1, 4))
        g22, g23 = gram(2, 2), gram(2, 3)
        s1 = g00 - g01
        k1 = g00 / s1
        rest = 1.0 - k1
        b1, f11 = g01, g11
        b2 = rest * g01 + k1 * g02
        f12 = rest * g11 + k1 * g12
        f2v2 = rest * g12 + k1 * g22
        f22 = rest * f12 + k1 * f2v2
        a1 = b1 - b2
        left1 = k1 * f11 / s1
        s2 = -k1 * (f12 - f11) - left1 * (b2 - b1)
        m2 = k1 - 1.0 - a1 / s1
        c22 = -k1 * f12 - left1 * b2
        alpha = 1.0 - c22 / s2
        beta = b2 / s1 - c22 * m2 / s2
        both = k1 + beta
        h1 = (1.0 - both) - alpha * rest
        h2 = both + alpha * rest - alpha * k1
        h3 = alpha * k1
        b3 = h1 * g01 + h2 * g02 + h3 * g03
        f13 = h1 * g11 + h2 * g12 + h3 * g13
        f23 = rest * f13 + k1 * (h1 * g12 + h2 * g22 + h3 * g23)
        a1 = b2 - b3
        a2 = -k1 * (f13 - f12) - left1 * (b3 - b2)
        l1 = (alpha * f12 + beta * f11) / s1
        l2 = (alpha * (f22 + m2 * f12) + beta * (f12 + m2 * f11)) / s2
        s3 = -(alpha * (f23 - f22) + beta * (f13 - f12)) + l1 * a1 + l2 * a2
        on2 = alpha - 1.0 - a2 / s2
        on1 = beta - a1 / s1 - a2 * m2 / s2
        c1 = -b3
        c2 = -k1 * f13 - left1 * b3
        c3 = -(alpha * f23 + beta * f13) + l1 * c1 + l2 * c2
        w3 = 1.0 - c3 / s3
        w2 = alpha - c2 / s2 - c3 * on2 / s3
        w1 = both - c1 / s1 - c2 * m2 / s2 - c3 * on1 / s3
        y1 = w1 + w2 * rest + w3 * h1
        y2 = w2 * k1 + w3 * h2
        y3 = w3 * h3

        def fill(row, _):
            out[row] = (vecs[0, row] + y1 * vecs[1, row]) + (y2 * vecs[2, row] + y3 * vecs[3, row])
            return 0

        lax.fori_loop(0, row_count, fill, 0)

        def blank(row, _):
            out[row] = jnp.zeros(out.shape[1:], F32)
            return 0

        lax.fori_loop(row_count, full_rows, blank, 0)

    @on(0)
    def _():
        send_halo(0, 0)
        send_rim(0)
        send_terms(0, 0)
        for copy in input_copies(0)[5:]:
            copy.wait()
        prepare(0)

    for level in range(1, BRANCHES):

        @on(level)
        def _(level=level):
            send_rim(level)
            for copy in input_copies(level):
                copy.wait()
            prepare(level)

    def body(turn, _):
        to = turn + 1
        later = turn > 0

        for level in range(BRANCHES):

            @pl.when(jnp.logical_and(branch == level, later))
            def _(level=level):
                send_terms(level, turn)

            @pl.when(jnp.logical_and(branch == level, later if level > 0 else turn >= 0))
            def _(level=level):
                convs_before(level, turn, to)

        @pl.when(turn == 1)
        def _():
            products([(0, 0), (0, 1), (1, 1)])

        @pl.when(turn == 2)
        def _():
            products([(0, 2), (1, 2), (2, 2)])

        for level in range(BRANCHES):

            @pl.when(jnp.logical_and(branch == level, turn == 0))
            def _(level=level):
                wait_rim(level)

            @pl.when(jnp.logical_and(branch == level, later if level > 0 else turn >= 0))
            def _(level=level):
                convs_after(level, turn, to)

            for when in range(ITERS):

                @pl.when(jnp.logical_and(branch == level, turn == when))
                def _(level=level, when=when):
                    finish(level, when)

        return 0

    lax.fori_loop(0, ITERS, body, 0)
    last_step()

    for level in range(BRANCHES):

        @on(level)
        def _(level=level):
            @pl.when(has_below)
            def _():
                rim_copy(level, True).wait_send()

            @pl.when(has_above)
            def _():
                rim_copy(level, False).wait_send()

            for turn in range(0 if level == 0 else 1, ITERS):
                for sends, copy, _ in halo_copies(level, turn):

                    @pl.when(sends)
                    def _(copy=copy):
                        copy.wait_send()

                for other in range(BRANCHES):
                    if other != level:
                        join_copy(level, other, turn).wait_send()

    pair_copy().wait_send()
    wait_all(took, sum_send.at[1])


def on_device(pieces, *args):
    full_rows, chans, width = args[5].shape[2:]
    across = min(4, pieces // 2)
    peers = pieces // 2 * BRANCHES - 1
    classes = args[0].shape[0]
    vmem = pltpu.VMEM

    def band_shape(level):
        size, many = BASE_CH << level, GROUP[level]
        return vmem((2, 3 * many * size, (many + 2) * size), BF16)

    def pair_shape(low, high):
        return vmem((ITERS, full_rows * BASE_CH >> (high - low), width >> high), BF16)

    pairs = [(0, 1), (0, 2), (0, 3), (1, 2), (1, 3), (2, 3)]
    scratch = (
        [
            vmem((classes, full_rows, width), BF16),
            vmem((full_rows, width), jnp.int32),
            vmem((full_rows, width), F32),
            vmem((classes, BASE_CH), BF16),
            vmem((full_rows, chans, width), BF16),
            vmem((full_rows + 2, chans, width), BF16),
            vmem((9, 256, 256), BF16),
            vmem((9, 256, 256), BF16),
            vmem((6, 256, 256), BF16),
        ]
        + [band_shape(level) for level in range(BRANCHES)]
        + [
            vmem((6, 256, 256), BF16),
            vmem((256, 128), BF16),
            vmem((1024, 256), BF16),
            vmem((1024, 128), BF16),
            vmem((128, 256), BF16),
            vmem((256, 1024), BF16),
            vmem((128, 1024), BF16),
            vmem((ITERS, full_rows + 4, chans, width), BF16),
            vmem((full_rows + 2, chans, width), BF16),
            vmem((ITERS + 1, full_rows, chans, width), F32),
        ]
        + [pair_shape(*pair) for pair in pairs] * 2
        + [
            vmem((1, 128), F32),
            vmem((1, 128), F32),
            vmem((1, 128), F32),
            vmem((peers, 1, 128), F32),
            pltpu.SemaphoreType.DMA((12,)),
            pltpu.SemaphoreType.DMA((2,)),
            pltpu.SemaphoreType.DMA((2,)),
            pltpu.SemaphoreType.DMA((ITERS, 4)),
            pltpu.SemaphoreType.DMA((ITERS, 4)),
            pltpu.SemaphoreType.DMA((ITERS, 4)),
            pltpu.SemaphoreType.DMA((ITERS, 4)),
            pltpu.SemaphoreType.DMA((2,)),
            pltpu.SemaphoreType.DMA((2,)),
        ]
    )
    result = pl.pallas_call(
        partial(kernel, pieces, across),
        out_shape=jax.ShapeDtypeStruct((full_rows, chans, width), F32),
        in_specs=[pl.BlockSpec(memory_space=pltpu.HBM)] * 9,
        out_specs=pl.BlockSpec(memory_space=pltpu.VMEM),
        scratch_shapes=scratch,
        compiler_params=pltpu.CompilerParams(
            collective_id=0, has_side_effects=True, vmem_limit_bytes=58 * 1024 * 1024
        ),
    )(*args[:3], args[3].T, *args[4:])
    return result[None, None]


def solution(mesh):
    placed = (
        P(None, "rows", None),
        P("rows", None),
        P("rows", None),
        P(),
        P("branch", "rows", None, None, None),
        P("branch", "rows", None, None, None),
        P("branch", None, None, None),
        P("branch", None, None, None),
        P(),
    )
    return jax.shard_map(
        partial(on_device, mesh.shape["rows"]),
        mesh=mesh,
        in_specs=placed,
        out_specs=P("branch", "rows", None, None, None),
        check_vma=False,
    )
```

time: 900 us -> 39.1 us (0.04); the launches traced: 887 us -> 38.9 us
  blocking collectives: 367 us -> 0 us
  starting transfers between devices: 185 us -> 0 us
  other arithmetic: 133 us -> 0 us
  matrix products: 76 us -> 0 us
  loops' own time: 56.9 us -> 0 us
  local copies, waits for them, and re-layouts: 47 us -> 2.31 us
  Pallas kernels: 0 us -> 36.6 us
  waiting for transfers between devices: 21.4 us -> 0 us
    psum x5 -> x0, blocking collectives: 367 us -> none  [the longest x2 162 us: on_device(): pair_sums = lax.psum(jnp.stack(pair_terms), ('rows', 'branch'))]
    all_to_all x3 -> x0, starting transfers between devices: 157 us -> none  [on_device(): lax.all_to_all(as_sent(outgoing), 'branch', split_axis=0, concat_axis=0,...]
    dot_general x64 -> x0, matrix products: 76 us -> none  [the longest x54 60.4 us: conv_level(): jnp.einsum('oi,roq->riq', weights[kernel_tap], window, preferred_element_...]
    reduce_sum x22 -> x0, other arithmetic: 70.9 us -> none  [the longest x12 38.1 us: pool_sum(): grid_map.reshape(height // factor, factor, channels, columns // factor, f...]
    another operation x9 -> x0, loops' own time: 56.9 us -> none  [the longest x3 55.1 us: on_device(): lax.switch(branch_level, [partial(send_level, position, join_weight) for...]
    pallas_call x0 -> x1, Pallas kernels: none -> 36.6 us  [on_device(): pl.pallas_call(partial(kernel, pieces, across), out_shape=jax.ShapeDtypeS...]
    convert_element_type x9 -> x0, other arithmetic: 28.2 us -> none  [the longest x3 11.4 us: contribute(): pooled = pool_sum(source.astype(jnp.float32), factor)]
    ppermute x12 -> x0, starting transfers between devices: 28 us -> none  [the longest x6 14.8 us: with_halo(): lax.ppermute(lax.slice_in_dim(block, block.shape[dim] - width, None, axis...]
  transfers between devices with their start and end apart: 15 -> 0, of which waited for: 6 -> 0; matrix products, arithmetic and copies ran while one was open for 9% -> 0% of each run, Pallas kernels for 0% -> 0%
where the time goes in v1:
time: 39.1 us; the launch traced here: 38.9 us
  Pallas kernels  36.6 us (94%)
  local copies, waits for them, and re-layouts  2.31 us (6%)
    pallas_call x1, Pallas kernels, on_device(): pl.pallas_call(partial(kernel, pieces, across), out_shape=jax.ShapeDtypeS...  36.6 us
    unnamed x1, local copies, waits for them, and re-layouts  2.31 us

profile of v1, /device:TPU:1, one launch (start us, length us, event | category | flops | bytes accessed | tf_op | source)
XLA Modules:
  0.0 38.9 jit_solution(17842099026565433220)
XLA Ops:
  0.0 36.6 %shard_map.91 = f32[8,32,1024]{2,1,0:T(8,128)} custom-call(bf16[19,8,1024]{2,1,0:T(8,128)(2,1)} %logits.1, s32[8,1024]{1,0:T(8,128)} %labels.1, f32[8,1024]{1,0:T(8,128)} %pixel_weight.1, bf16[19,32]{1,0:T(8,128)(2,1)} %bitcast.3, bf16[1,1,8,32,1024]{4,3,2,1,0:T(8,128)(2,1)} %deriv_inner.1, bf16[1,1,8,32,1024]{4,3,2,1,0:T(8,128)(2,1)} %deriv_outer.1, ...), custom_call_target="tpu_custom_call" | custom-call | tf_op jit(solution)/shard_map/pallas_call | solution.py:765
  36.6 2.3 %copy.11 = f32[1,1,8,32,1024]{4,3,2,1,0:T(8,128)} copy(f32[1,1,8,32,1024]{4,3,2,1,0:T(8,128)} %bitcast.2) | data formatting | bytes 2097152

commit v2 on v1

--- a/solution.py
+++ b/solution.py
@@ -93,9 +93,8 @@
     take13,
     take23,
     part,
-    took_pair,
-    part_pair,
     took,
+    known,
     in_sem,
     rim_send,
     rim_recv,
@@ -122,21 +121,31 @@
         return full_rows >> level, BASE_CH << level, width >> level, 1 << level
 
     def hops(offset):
-        return sum(min(step, size - step) for step, size in zip(offset, (across, deep, BRANCHES)))
+        far = sum(min(step, size - step) for step, size in zip(offset[1:], (across, deep, BRANCHES)))
+        return far + 0.3 * offset[0]
 
     offsets = [
-        (x, z, y) for x in range(across) for z in range(deep) for y in range(BRANCHES) if x or z or y
+        (c, x, z, y)
+        for c in range(2)
+        for x in range(across)
+        for z in range(deep)
+        for y in range(BRANCHES)
+        if c or x or z or y
     ]
     offsets.sort(key=hops, reverse=True)
-    partner = (piece + 1 - 2 * core, branch)
-
-    def chip_peer(offset):
-        x = lax.rem(chip_x + offset[0], across)
-        z = lax.rem(chip_z + offset[1], deep)
-        return ((z * across + x) * 2 + core, lax.rem(branch + offset[2], BRANCHES))
-
+
+    def peer(offset):
+        c = lax.rem(core + offset[0], 2)
+        x = lax.rem(chip_x + offset[1], across)
+        z = lax.rem(chip_z + offset[2], deep)
+        return ((z * across + x) * 2 + c, lax.rem(branch + offset[3], BRANCHES))
+
+    along_x = [peer((0, step, 0, 0)) for step in range(1, across)]
+    along_z = [peer((0, 0, step, 0)) for step in range(1, deep)]
+    along_y = [peer((0, 0, 0, step)) for step in range(1, BRANCHES)]
+    partner = peer((1, 0, 0, 0))
     near = [(lax.rem(piece + step, pieces), branch) for step in (1, 2, pieces - 2, pieces - 1)]
-    greeted = [chip_peer(offset) for offset in offsets] + near + [partner]
+    greeted = near + along_z + along_y + along_x + [partner]
 
     def on(level):
         return pl.when(branch == level)
@@ -167,8 +176,8 @@
                 copy.start()
 
     barrier = pltpu.get_barrier_semaphore()
-    for peer in greeted:
-        pl.semaphore_signal(barrier, inc=1, device_id=peer, device_id_type=MESH)
+    for other in greeted:
+        pl.semaphore_signal(barrier, inc=1, device_id=other, device_id_type=MESH)
 
     for ref, factor in ((pool2, 2), (pool4, 4), (pool8, 8)):
         row, col = iotas(ref.shape)
@@ -264,9 +273,26 @@
             vecs[0, row] = jnp.zeros(vecs.shape[2:], F32)
             return 0
 
-        lax.fori_loop(0, row_count, clear, 0)
+        lax.fori_loop(0, full_rows, clear, 0)
+
+        def blank(row, _):
+            out[row] = jnp.zeros(out.shape[1:], F32)
+            return 0
+
+        lax.fori_loop(row_count, full_rows, blank, 0)
 
     pl.semaphore_wait(barrier, len(greeted))
+
+    circles = (along_x, along_y, [partner])
+
+    def tell(at):
+        for other in circles[at]:
+            pl.semaphore_signal(known.at[at], inc=1, device_id=other, device_id_type=MESH)
+
+    def hear(at):
+        pl.semaphore_wait(known.at[at], len(circles[at]))
+
+    tell(0)
 
     def rim_copy(level, below):
         rows = sizes(level)[0]
@@ -540,24 +566,15 @@
 
     part[...] = jnp.zeros(part.shape, F32)
 
-    def pair_copy():
-        return pltpu.make_async_remote_copy(
-            part, took_pair, sum_send.at[0], sum_recv.at[0], device_id=partner, device_id_type=MESH
-        )
-
     def last_step():
         products([(0, 3), (1, 3), (2, 3)])
-        copy = pair_copy()
-        copy.start()
-        copy.wait_recv()
-        part_pair[...] = part[...] + took_pair[...]
+        hear(2)
         for at, offset in enumerate(offsets):
             pltpu.make_async_remote_copy(
-                part_pair, took.at[at], sum_send.at[1], sum_recv.at[1],
-                device_id=chip_peer(offset), device_id_type=MESH,
+                part, took.at[at], sum_send, sum_recv, device_id=peer(offset), device_id_type=MESH
             ).start()
-        wait_all(took, sum_recv.at[1])
-        sums = part_pair[...] + jnp.sum(took[...], axis=0)
+        wait_all(took, sum_recv)
+        sums = part[...] + jnp.sum(took[...], axis=0)
 
         def gram(left, right):
             at = 3 * left + right
@@ -611,12 +628,6 @@
 
         lax.fori_loop(0, row_count, fill, 0)
 
-        def blank(row, _):
-            out[row] = jnp.zeros(out.shape[1:], F32)
-            return 0
-
-        lax.fori_loop(row_count, full_rows, blank, 0)
-
     @on(0)
     def _():
         send_halo(0, 0)
@@ -639,6 +650,13 @@
         to = turn + 1
         later = turn > 0
 
+        for at in range(2):
+
+            @pl.when(turn == at + 1)
+            def _(at=at):
+                hear(at)
+                tell(at + 1)
+
         for level in range(BRANCHES):
 
             @pl.when(jnp.logical_and(branch == level, later))
@@ -701,14 +719,13 @@
                     if other != level:
                         join_copy(level, other, turn).wait_send()
 
-    pair_copy().wait_send()
-    wait_all(took, sum_send.at[1])
+    wait_all(took, sum_send)
 
 
 def on_device(pieces, *args):
     full_rows, chans, width = args[5].shape[2:]
     across = min(4, pieces // 2)
-    peers = pieces // 2 * BRANCHES - 1
+    peers = pieces * BRANCHES - 1
     classes = args[0].shape[0]
     vmem = pltpu.VMEM
 
@@ -748,9 +765,8 @@
         + [pair_shape(*pair) for pair in pairs] * 2
         + [
             vmem((1, 128), F32),
-            vmem((1, 128), F32),
-            vmem((1, 128), F32),
             vmem((peers, 1, 128), F32),
+            pltpu.SemaphoreType.REGULAR((3,)),
             pltpu.SemaphoreType.DMA((12,)),
             pltpu.SemaphoreType.DMA((2,)),
             pltpu.SemaphoreType.DMA((2,)),
@@ -758,8 +774,8 @@
             pltpu.SemaphoreType.DMA((ITERS, 4)),
             pltpu.SemaphoreType.DMA((ITERS, 4)),
             pltpu.SemaphoreType.DMA((ITERS, 4)),
-            pltpu.SemaphoreType.DMA((2,)),
-            pltpu.SemaphoreType.DMA((2,)),
+            pltpu.SemaphoreType.DMA,
+            pltpu.SemaphoreType.DMA,
         ]
     )
     result = pl.pallas_call(
@@ -769,9 +785,9 @@
         out_specs=pl.BlockSpec(memory_space=pltpu.VMEM),
         scratch_shapes=scratch,
         compiler_params=pltpu.CompilerParams(
-            collective_id=0, has_side_effects=True, vmem_limit_bytes=58 * 1024 * 1024
+            collective_id=0, has_side_effects=True, vmem_limit_bytes=40 * 1024 * 1024
         ),
-    )(*args[:3], args[3].T, *args[4:])
+    )(*[pltpu.with_memory_space_constraint(arg, pltpu.HBM) for arg in (*args[:3], args[3].T, *args[4:])])
     return result[None, None]
 
 

time: 39.1 us -> 35.3 us (0.903)
  Pallas kernels: 36.6 us -> 34.2 us
  local copies, waits for them, and re-layouts: 2.31 us -> 0.97 us
    pallas_call x1, Pallas kernels: 36.6 us -> 34.2 us  [on_device(): pl.pallas_call(partial(kernel, pieces, across), out_shape=jax.ShapeDtypeS...]
    unnamed x1, local copies, waits for them, and re-layouts: 2.31 us -> 0.97 us
where the time goes in v2:
time: 35.3 us; the launch traced here: 35.1 us
  Pallas kernels  34.2 us (97%)
  local copies, waits for them, and re-layouts  0.97 us (3%)
    pallas_call x1, Pallas kernels, on_device(): pl.pallas_call(partial(kernel, pieces, across), out_shape=jax.ShapeDtypeS...  34.2 us
    unnamed x1, local copies, waits for them, and re-layouts  0.97 us

profile of v2, /device:TPU:1, one launch (start us, length us, event | category | flops | bytes accessed | tf_op | source)
XLA Modules:
  0.0 35.1 jit_solution(911038868239269557)
XLA Ops:
  0.0 34.2 %shard_map.91 = f32[8,32,1024]{2,1,0:T(8,128)S(1)} custom-call(bf16[19,8,1024]{2,1,0:T(8,128)(2,1)} %logits.1, s32[8,1024]{1,0:T(8,128)} %labels.1, f32[8,1024]{1,0:T(8,128)} %pixel_weight.1, bf16[19,32]{1,0:T(8,128)(2,1)} %bitcast.3, bf16[1,1,8,32,1024]{4,3,2,1,0:T(8,128)(2,1)} %deriv_inner.1, bf16[1,1,8,32,1024]{4,3,2,1,0:T(8,128)(2,1)} %deriv_outer.1, ...), custom_call_target="tpu_custom_call" | custom-call | tf_op jit(solution)/shard_map/pallas_call | solution.py:781
  34.2 1.0 %copy.11 = f32[1,1,8,32,1024]{4,3,2,1,0:T(8,128)} copy(f32[1,1,8,32,1024]{4,3,2,1,0:T(8,128)S(1)} %bitcast.2) | data formatting | bytes 2097152

commit v3 on v2

--- a/solution.py
+++ b/solution.py
@@ -120,19 +120,9 @@
     def sizes(level):
         return full_rows >> level, BASE_CH << level, width >> level, 1 << level
 
-    def hops(offset):
-        far = sum(min(step, size - step) for step, size in zip(offset[1:], (across, deep, BRANCHES)))
-        return far + 0.3 * offset[0]
-
-    offsets = [
-        (c, x, z, y)
-        for c in range(2)
-        for x in range(across)
-        for z in range(deep)
-        for y in range(BRANCHES)
-        if c or x or z or y
-    ]
-    offsets.sort(key=hops, reverse=True)
+    spread = [(there, level) for there in range(pieces) for level in range(BRANCHES)]
+    spread.sort(key=lambda at: at[0] // (2 * across) + 0.7 * (at[0] // 2 % across) + at[1])
+    others = took.at[pl.ds(0, pieces * BRANCHES - 1)]
 
     def peer(offset):
         c = lax.rem(core + offset[0], 2)
@@ -378,11 +368,11 @@
     def grid_rows(load, slots, level):
         return jnp.concatenate([part for slot in slots for part in chunks(load(slot), level)], axis=0)
 
-    def send_terms(level, turn):
+    def send_terms(level, turn, coarser=None):
         rows, chans, cols, _ = sizes(level)
         load = lambda slot: scaled[turn, slot]
         own = grid_rows(load, range(2, 2 + rows), level)
-        for other in range(level + 1, BRANCHES):
+        for other in coarser or range(level + 1, BRANCHES):
             factor = 1 << (other - level)
             height, less = rows // factor, cols // factor
             ref = gives[(level, other)]
@@ -569,12 +559,19 @@
     def last_step():
         products([(0, 3), (1, 3), (2, 3)])
         hear(2)
-        for at, offset in enumerate(offsets):
-            pltpu.make_async_remote_copy(
-                part, took.at[at], sum_send, sum_recv, device_id=peer(offset), device_id_type=MESH
-            ).start()
-        wait_all(took, sum_recv)
-        sums = part[...] + jnp.sum(took[...], axis=0)
+        mine = piece * BRANCHES + branch
+        for there, level in spread:
+
+            @pl.when(jnp.logical_or(piece != there, branch != level))
+            def _(there=there, level=level):
+                pltpu.make_async_remote_copy(
+                    part, took.at[mine], sum_send, sum_recv,
+                    device_id=(jnp.int32(there), jnp.int32(level)), device_id_type=MESH,
+                ).start()
+
+        wait_all(others, sum_recv)
+        took[mine] = part[...]
+        sums = jnp.sum(took[...], axis=0)
 
         def gram(left, right):
             at = 3 * left + right
@@ -631,8 +628,8 @@
     @on(0)
     def _():
         send_halo(0, 0)
+        send_terms(0, 0, (3, 2, 1))
         send_rim(0)
-        send_terms(0, 0)
         for copy in input_copies(0)[5:]:
             copy.wait()
         prepare(0)
@@ -719,13 +716,12 @@
                     if other != level:
                         join_copy(level, other, turn).wait_send()
 
-    wait_all(took, sum_send)
+    wait_all(others, sum_send)
 
 
 def on_device(pieces, *args):
     full_rows, chans, width = args[5].shape[2:]
     across = min(4, pieces // 2)
-    peers = pieces * BRANCHES - 1
     classes = args[0].shape[0]
     vmem = pltpu.VMEM
 
@@ -765,7 +761,7 @@
         + [pair_shape(*pair) for pair in pairs] * 2
         + [
             vmem((1, 128), F32),
-            vmem((peers, 1, 128), F32),
+            vmem((pieces * BRANCHES, 1, 128), F32),
             pltpu.SemaphoreType.REGULAR((3,)),
             pltpu.SemaphoreType.DMA((12,)),
             pltpu.SemaphoreType.DMA((2,)),

time: 35.3 us -> 34.8 us (0.986)
  Pallas kernels: 34.2 us -> 33.7 us
    pallas_call x1, Pallas kernels: 34.2 us -> 33.7 us  [on_device(): pl.pallas_call(partial(kernel, pieces, across), out_shape=jax.ShapeDtypeS...]
where the time goes in v3:
time: 34.8 us; the launch traced here: 34.7 us
  Pallas kernels  33.7 us (97%)
  local copies, waits for them, and re-layouts  0.97 us (3%)
    pallas_call x1, Pallas kernels, on_device(): pl.pallas_call(partial(kernel, pieces, across), out_shape=jax.ShapeDtypeS...  33.7 us
    unnamed x1, local copies, waits for them, and re-layouts  0.97 us

profile of v3, /device:TPU:1, one launch (start us, length us, event | category | flops | bytes accessed | tf_op | source)
XLA Modules:
  0.0 34.7 jit_solution(6919320056713396374)
XLA Ops:
  0.0 33.7 %shard_map.91 = f32[8,32,1024]{2,1,0:T(8,128)S(1)} custom-call(bf16[19,8,1024]{2,1,0:T(8,128)(2,1)} %logits.1, s32[8,1024]{1,0:T(8,128)} %labels.1, f32[8,1024]{1,0:T(8,128)} %pixel_weight.1, bf16[19,32]{1,0:T(8,128)(2,1)} %bitcast.3, bf16[1,1,8,32,1024]{4,3,2,1,0:T(8,128)(2,1)} %deriv_inner.1, bf16[1,1,8,32,1024]{4,3,2,1,0:T(8,128)(2,1)} %deriv_outer.1, ...), custom_call_target="tpu_custom_call" | custom-call | tf_op jit(solution)/shard_map/pallas_call | solution.py:777
  33.7 1.0 %copy.11 = f32[1,1,8,32,1024]{4,3,2,1,0:T(8,128)} copy(f32[1,1,8,32,1024]{4,3,2,1,0:T(8,128)S(1)} %bitcast.2) | data formatting | bytes 2097152

commit v4 on v3

--- a/solution.py
+++ b/solution.py
@@ -523,6 +523,7 @@
         to = turn + 1
         others = [other for other in range(BRANCHES) if other != level and (turn > 0 or other == 0)]
         terms = [term_rows(level, other, turn) for other in others]
+        dots = [jnp.zeros((8, cols), F32)] * ITERS
         for done, row in enumerate(order[level]):
             for at in range(factor):
                 lanes = slice(at * cols, (at + 1) * cols)
@@ -532,10 +533,16 @@
                 for more in parts[1:]:
                     value = value + more
                 vecs[to, row, :, lanes] = value
-                if to < ITERS:
+                if to == ITERS:
+                    for left in range(ITERS):
+                        prod = vecs[left, row, :, lanes] * value
+                        dots[left] = dots[left] + ((prod[0:8] + prod[8:16]) + (prod[16:24] + prod[24:32]))
+                else:
                     scaled[to, 2 + row, :, lanes] = (outer[row, :, lanes].astype(F32) * value).astype(BF16)
             if to < ITERS and done + 1 == rims[level]:
                 send_halo(level, to)
+        if to == ITERS:
+            collect(dots, [(left, ITERS) for left in range(ITERS)])
 
     def products(pairs):
         def step(row, sums):
@@ -546,7 +553,9 @@
             return tuple(result)
 
         zero = jnp.zeros((8, width), F32)
-        sums = lax.fori_loop(0, row_count, step, (zero,) * len(pairs))
+        collect(lax.fori_loop(0, row_count, step, (zero,) * len(pairs)), pairs)
+
+    def collect(sums, pairs):
         lane = lax.broadcasted_iota(jnp.int32, part.shape, 1)
         row_of = part[...]
         for value, (left, right) in zip(sums, pairs):
@@ -557,7 +566,6 @@
     part[...] = jnp.zeros(part.shape, F32)
 
     def last_step():
-        products([(0, 3), (1, 3), (2, 3)])
         hear(2)
         mine = piece * BRANCHES + branch
         for there, level in spread:
@@ -581,7 +589,8 @@
         g11, g12, g13 = (gram(1, at) for at in range(1, 4))
         g22, g23 = gram(2, 2), gram(2, 3)
         s1 = g00 - g01
-        k1 = g00 / s1
+        r1 = 1.0 / s1
+        k1 = g00 * r1
         rest = 1.0 - k1
         b1, f11 = g01, g11
         b2 = rest * g01 + k1 * g02
@@ -589,12 +598,13 @@
         f2v2 = rest * g12 + k1 * g22
         f22 = rest * f12 + k1 * f2v2
         a1 = b1 - b2
-        left1 = k1 * f11 / s1
+        left1 = k1 * f11 * r1
         s2 = -k1 * (f12 - f11) - left1 * (b2 - b1)
-        m2 = k1 - 1.0 - a1 / s1
+        r2 = 1.0 / s2
+        m2 = k1 - 1.0 - a1 * r1
         c22 = -k1 * f12 - left1 * b2
-        alpha = 1.0 - c22 / s2
-        beta = b2 / s1 - c22 * m2 / s2
+        alpha = 1.0 - c22 * r2
+        beta = b2 * r1 - c22 * r2 * m2
         both = k1 + beta
         h1 = (1.0 - both) - alpha * rest
         h2 = both + alpha * rest - alpha * k1
@@ -604,17 +614,19 @@
         f23 = rest * f13 + k1 * (h1 * g12 + h2 * g22 + h3 * g23)
         a1 = b2 - b3
         a2 = -k1 * (f13 - f12) - left1 * (b3 - b2)
-        l1 = (alpha * f12 + beta * f11) / s1
-        l2 = (alpha * (f22 + m2 * f12) + beta * (f12 + m2 * f11)) / s2
+        l1 = (alpha * f12 + beta * f11) * r1
+        l2 = (alpha * (f22 + m2 * f12) + beta * (f12 + m2 * f11)) * r2
         s3 = -(alpha * (f23 - f22) + beta * (f13 - f12)) + l1 * a1 + l2 * a2
-        on2 = alpha - 1.0 - a2 / s2
-        on1 = beta - a1 / s1 - a2 * m2 / s2
+        r3 = 1.0 / s3
+        on2 = alpha - 1.0 - a2 * r2
+        on1 = beta - a1 * r1 - a2 * r2 * m2
         c1 = -b3
         c2 = -k1 * f13 - left1 * b3
         c3 = -(alpha * f23 + beta * f13) + l1 * c1 + l2 * c2
-        w3 = 1.0 - c3 / s3
-        w2 = alpha - c2 / s2 - c3 * on2 / s3
-        w1 = both - c1 / s1 - c2 * m2 / s2 - c3 * on1 / s3
+        c3 = c3 * r3
+        w3 = 1.0 - c3
+        w2 = alpha - c2 * r2 - c3 * on2
+        w1 = both - c1 * r1 - c2 * r2 * m2 - c3 * on1
         y1 = w1 + w2 * rest + w3 * h1
         y2 = w2 * k1 + w3 * h2
         y3 = w3 * h3

time: 34.8 us -> 34.7 us (level)
  no operation moved by 1% of the time
where the time goes in v4:
time: 34.7 us; the launch traced here: 34.6 us
  Pallas kernels  33.6 us (97%)
  local copies, waits for them, and re-layouts  0.97 us (3%)
    pallas_call x1, Pallas kernels, on_device(): pl.pallas_call(partial(kernel, pieces, across), out_shape=jax.ShapeDtypeS...  33.6 us
    unnamed x1, local copies, waits for them, and re-layouts  0.97 us

profile of v4, /device:TPU:1, one launch (start us, length us, event | category | flops | bytes accessed | tf_op | source)
XLA Modules:
  0.0 34.6 jit_solution(14466534747443438741)
XLA Ops:
  0.0 33.6 %shard_map.91 = f32[8,32,1024]{2,1,0:T(8,128)S(1)} custom-call(bf16[19,8,1024]{2,1,0:T(8,128)(2,1)} %logits.1, s32[8,1024]{1,0:T(8,128)} %labels.1, f32[8,1024]{1,0:T(8,128)} %pixel_weight.1, bf16[19,32]{1,0:T(8,128)(2,1)} %bitcast.3, bf16[1,1,8,32,1024]{4,3,2,1,0:T(8,128)(2,1)} %deriv_inner.1, bf16[1,1,8,32,1024]{4,3,2,1,0:T(8,128)(2,1)} %deriv_outer.1, ...), custom_call_target="tpu_custom_call" | custom-call | tf_op jit(solution)/shard_map/pallas_call | solution.py:789
  33.6 1.0 %copy.11 = f32[1,1,8,32,1024]{4,3,2,1,0:T(8,128)} copy(f32[1,1,8,32,1024]{4,3,2,1,0:T(8,128)S(1)} %bitcast.2) | data formatting | bytes 2097152

commit v5 on v4

--- a/solution.py
+++ b/solution.py
@@ -372,6 +372,16 @@
         rows, chans, cols, _ = sizes(level)
         load = lambda slot: scaled[turn, slot]
         own = grid_rows(load, range(2, 2 + rows), level)
+        for other in reversed(range(level)):
+            few = BASE_CH << other
+            factor = 1 << (level - other)
+            scale = few ** (-0.5) / (factor * factor)
+            ref = gives[(other, level)]
+            matrix = mix[other, :few, :chans]
+            for row in range(rows):
+                mixed = dot(matrix, own[row * chans : (row + 1) * chans])
+                ref[turn, row * few : (row + 1) * few, :] = (mixed * scale).astype(BF16)
+            join_copy(level, other, turn).start()
         for other in coarser or range(level + 1, BRANCHES):
             factor = 1 << (other - level)
             height, less = rows // factor, cols // factor
@@ -390,16 +400,6 @@
                         start = (row * factor + extra) * chans
                         summed = summed + part[start : start + chans]
                     ref[turn, row * chans : (row + 1) * chans, at * span : (at + 1) * span] = summed.astype(BF16)
-            join_copy(level, other, turn).start()
-        for other in range(level):
-            few = BASE_CH << other
-            factor = 1 << (level - other)
-            scale = few ** (-0.5) / (factor * factor)
-            ref = gives[(other, level)]
-            matrix = mix[other, :few, :chans]
-            for row in range(rows):
-                mixed = dot(matrix, own[row * chans : (row + 1) * chans])
-                ref[turn, row * few : (row + 1) * few, :] = (mixed * scale).astype(BF16)
             join_copy(level, other, turn).start()
 
     def conv(level, which, load, first, many):
@@ -521,7 +521,7 @@
     def finish(level, turn):
         _, _, cols, factor = sizes(level)
         to = turn + 1
-        others = [other for other in range(BRANCHES) if other != level and (turn > 0 or other == 0)]
+        others = [other for other in ((3, 2, 1), (3, 2, 0), (3, 0, 1), (0, 1, 2))[level] if turn > 0 or other == 0]
         terms = [term_rows(level, other, turn) for other in others]
         dots = [jnp.zeros((8, cols), F32)] * ITERS
         for done, row in enumerate(order[level]):

time: 34.7 us -> 34.2 us (0.986)
  Pallas kernels: 33.6 us -> 33.1 us
    pallas_call x1, Pallas kernels: 33.6 us -> 33.1 us  [on_device(): pl.pallas_call(partial(kernel, pieces, across), out_shape=jax.ShapeDtypeS...]
where the time goes in v5:
time: 34.2 us; the launch traced here: 34.1 us
  Pallas kernels  33.1 us (97%)
  local copies, waits for them, and re-layouts  0.97 us (3%)
    pallas_call x1, Pallas kernels, on_device(): pl.pallas_call(partial(kernel, pieces, across), out_shape=jax.ShapeDtypeS...  33.1 us
    unnamed x1, local copies, waits for them, and re-layouts  0.97 us

profile of v5, /device:TPU:1, one launch (start us, length us, event | category | flops | bytes accessed | tf_op | source)
XLA Modules:
  0.0 34.1 jit_solution(9990299153668805980)
XLA Ops:
  0.0 33.1 %shard_map.91 = f32[8,32,1024]{2,1,0:T(8,128)S(1)} custom-call(bf16[19,8,1024]{2,1,0:T(8,128)(2,1)} %logits.1, s32[8,1024]{1,0:T(8,128)} %labels.1, f32[8,1024]{1,0:T(8,128)} %pixel_weight.1, bf16[19,32]{1,0:T(8,128)(2,1)} %bitcast.3, bf16[1,1,8,32,1024]{4,3,2,1,0:T(8,128)(2,1)} %deriv_inner.1, bf16[1,1,8,32,1024]{4,3,2,1,0:T(8,128)(2,1)} %deriv_outer.1, ...), custom_call_target="tpu_custom_call" | custom-call | tf_op jit(solution)/shard_map/pallas_call | solution.py:789
  33.1 1.0 %copy.11 = f32[1,1,8,32,1024]{4,3,2,1,0:T(8,128)} copy(f32[1,1,8,32,1024]{4,3,2,1,0:T(8,128)S(1)} %bitcast.2) | data formatting | bytes 2097152
